TPU v7x, 32 devices: a whole 2x2x4 slice. The times are simulated.
32 devices in a mesh: groups: 2 (over y), ctx: 4 (over z), head: 2 (over x), rep: 2 (over core).
Axes of the slice: x: 2, y: 2, z: 4, core: 2. Of those that a mesh axis runs over, the one named last changes fastest.
Arguments:
- queries: bfloat16 [2048, 8192], P(('groups', 'rep'), 'head'), parts along dimension 0, may hold values from -6 to 6
- cached_keys: bfloat16 [32768, 1024], P(('groups', 'ctx'), 'head'), parts along dimension 0, may hold values from -6 to 6
- cached_values: bfloat16 [32768, 1024], P(('groups', 'ctx'), 'head'), parts along dimension 0, may hold values from -6 to 6
- pattern: int32 [16, 16], P(('groups', 'rep')), parts along dimension 0, may hold values from 0 to 127, as said below
- out_weight: bfloat16 [8192, 8192], P('head', 'ctx'), may hold values from -1.1953125 to 1.1953125
Outputs:
- projected: bfloat16 [2048, 8192], P(('groups', 'rep'), ('ctx', 'head')), parts along dimension 0
There are 2 independent parts, one for each index of `groups`. A program takes and returns all parts, laid end to end along the dimension named above; an argument that names none is the same for every part. Nothing has to cross between parts.
Inputs may be any that keep to these rules, and one draw needn't show every extreme that they name: Each row of pattern names 16 different key blocks; no row names more than 8 blocks among blocks k * 32 to (k + 1) * 32 - 1 for any k, and every row names exactly 8 in some such range.
All inputs are finite; a program needn't handle non-finite values.
Results may differ from a plain program's by a relative error of at most 0.0055.
Values may be sent and summed in bfloat16 or wider, within the bound.
A program may use at most 128 MiB of HBM per device.

v0:
```python
import jax
import jax.numpy as jnp
from jax import lax
from jax.sharding import PartitionSpec as P

HEADS = 64
KV_HEADS = 8
HEAD_DIM = 128
BLOCK = 128
CAP = 8


def shards(queries, cached_keys, cached_values, pattern, out_weight):
    shard_index = lax.axis_index("ctx")
    query_count, query_width = queries.shape
    cache_rows, cache_width = cached_keys.shape
    heads_kv = cache_width // HEAD_DIM
    group_size = HEADS // KV_HEADS
    heads_here = heads_kv * group_size
    local_blocks = cache_rows // BLOCK
    score_scale = HEAD_DIM ** (-0.5)
    key_blocks = cached_keys.reshape(local_blocks, BLOCK, cache_width)
    value_blocks = cached_values.reshape(local_blocks, BLOCK, cache_width)
    query_blocks = queries.reshape(query_count // BLOCK, BLOCK, heads_kv, group_size, HEAD_DIM)
    slot_ids = jnp.arange(CAP, dtype=jnp.int32)

    def attend(inputs):
        query_block, chosen_list = inputs
        local_block = chosen_list - shard_index * local_blocks
        in_shard = (local_block >= 0) & (local_block < local_blocks)
        slot_rank = jnp.cumsum(in_shard.astype(jnp.int32)) - 1
        picked = in_shard[:, None] & (slot_rank[:, None] == slot_ids[None, :])
        chosen = jnp.sum(jnp.where(picked, local_block[:, None], 0), axis=0)
        slot_live = jnp.any(picked, axis=0)
        key_block = key_blocks[chosen].reshape(CAP * BLOCK, heads_kv, HEAD_DIM)
        value_block = value_blocks[chosen].reshape(CAP * BLOCK, heads_kv, HEAD_DIM)
        scores = (
            jnp.einsum("rkgd,skd->kgrs", query_block, key_block, preferred_element_type=jnp.float32)
            * score_scale
        )
        key_live = jnp.repeat(slot_live, BLOCK)
        masked = jnp.where(key_live, scores, jnp.float32(-1e30))
        row_top = masked.max(axis=-1)
        weights = jnp.where(key_live, jnp.exp(masked - row_top[..., None]), 0.0)
        row_total = weights.sum(axis=-1)
        mixed = jnp.einsum(
            "kgrs,skd->rkgd",
            weights.astype(jnp.bfloat16),
            value_block,
            preferred_element_type=jnp.float32,
        )
        return (
            mixed.reshape(BLOCK, heads_here * HEAD_DIM),
            row_top.transpose(2, 0, 1).reshape(BLOCK, heads_here),
            row_total.transpose(2, 0, 1).reshape(BLOCK, heads_here),
        )

    mixed_all, top_all, total_all = lax.map(attend, (query_blocks, pattern))
    mixed_all = mixed_all.reshape(query_count, query_width)
    top_all = top_all.reshape(query_count, heads_here)
    total_all = total_all.reshape(query_count, heads_here)
    sources = lax.axis_size("ctx")
    got_mixed, got_top, got_total = (
        lax.all_to_all(mixed_all, "ctx", split_axis=0, concat_axis=0, tiled=True),
        lax.all_to_all(top_all, "ctx", split_axis=0, concat_axis=0, tiled=True),
        lax.all_to_all(total_all, "ctx", split_axis=0, concat_axis=0, tiled=True),
    )
    got_mixed = got_mixed.reshape(sources, -1, heads_here, HEAD_DIM)
    got_top = got_top.reshape(sources, -1, heads_here)
    got_total = got_total.reshape(sources, -1, heads_here)
    row_peak = got_top.max(axis=0)
    rescale = jnp.exp(got_top - row_peak[None])
    summed = jnp.sum(got_mixed * rescale[..., None], axis=0)
    row_norm = jnp.sum(got_total * rescale, axis=0)
    attended = (summed / row_norm[:, :, None]).reshape(-1, query_width).astype(jnp.bfloat16)
    partial_out = jnp.dot(
        lax.all_gather(attended, "ctx", axis=0, tiled=True),
        out_weight,
        preferred_element_type=jnp.float32,
    )
    return lax.psum_scatter(partial_out, "head", scatter_dimension=1, tiled=True).astype(
        jnp.bfloat16
    )


def solution(mesh):
    return jax.shard_map(
        shards,
        mesh=mesh,
        in_specs=(
            P(("groups", "rep"), "head"),
            P(("groups", "ctx"), "head"),
            P(("groups", "ctx"), "head"),
            P(("groups", "rep"), None),
            P("head", "ctx"),
        ),
        out_specs=P(("groups", "rep"), ("ctx", "head")),
        check_vma=False,
    )
```

profile of v0, /device:TPU:0, one launch (start us, length us, event | category | flops | bytes accessed | tf_op | source)
XLA Modules:
  0.0 489.8 jit_solution(8552353917670141970)
XLA Ops:
  6.5 5.4 %copy.36 = bf16[64,8,32,128]{3,2,1,0:T(8,128)(2,1)} copy(bf16[64,8,32,128]{3,1,2,0:T(8,128)(2,1)} %bitcast.89) | data formatting | bytes 8388608
  12.0 109.1 %while.17 = (s32[]{:T(128)}, f32[4,128,4096]{1,2,0:T(8,128)}, f32[4,128,32]{1,2,0:T(8,128)S(1)}, f32[4,128,32]{1,2,0:T(8,128)S(1)}, s32[4,16]{1,0:T(4,128)}, /*i...) while((s32[]{:T(128)}, f32[4,128,4096]{1,2,0:T(8,128)}, ...), condition=%wide.region_6.7_spmd.clone, body=%wide.region_0.6_spmd.clone.sunk | while | flops 2202003712 | bytes 137504496 | solution.py:58
  12.0 0.7 compare_and_fusion.2
  12.9 0.1 select_reduce_fusion.2
  13.1 2.8 gather_fusion
  15.9 0.3 reshape.193
  16.2 0.1 fusion.37
  16.4 1.3 constant_dynamic-slice_fusion.3
  17.7 3.1 bitcast_reduce_fusion.2
  20.8 5.0 %fusion.40 = f32[4,8,128]{2,1,0:T(8,128)S(1)} fusion(f32[4,1024,128,8]{2,1,3,0:T(8,128)S(1)} %get-tuple-element.282, f32[4,8,128]{2,1,0:T(8,128)S(1)} %get-tuple-element.283, pred[1024]{0:T(1024)(128)(4,1)S(1)} %broadcast_bitcast_fusion.2), kind=kLoop, calls=%fused_computation.8.clone.1 | loop fusion | flops 20967424 | bytes 16811008 | tf_op jit(solution)/shard_map/while/body/eval_jaxpr/reduce_sum | solution.py:45
  25.8 0.7 copy-done
  26.5 2.8 gather_fusion.1
  29.3 0.3 reshape.194
  29.6 8.2 %fusion.39 = f32[4,128,8,128]{3,1,2,0:T(8,128)S(1)} fusion(f32[4,1024,128,8]{2,1,3,0:T(8,128)} %copy-done, f32[4,8,128]{2,1,0:T(8,128)S(1)} %get-tuple-element.283, pred[1024]{0:T(1024)(128)(4,1)S(1)} %broadcast_bitcast_fusion.2, bf16[1024,4,128,1]{2,1,0,3:T(4,128)(2,1)S(1)} %bitcast.85), kind=kOutput, calls=%fused_computation.10.clone.1 | convolution fusion | flops 1094713344 | bytes 19940352 | tf_op jit(solution)/shard_map/while/body/eval_jaxpr/kgrs,skd->rkgd/dot_general | solution.py:46
  37.8 1.5 constant_dynamic-update-slice_fusion.2
  39.3 0.7 compare_and_fusion.2
  40.2 0.1 select_reduce_fusion.2
  40.3 2.8 gather_fusion
  43.2 0.3 reshape.193
  43.5 0.1 fusion.37
  43.6 1.3 constant_dynamic-slice_fusion.3
  44.9 3.1 bitcast_reduce_fusion.2
  48.1 5.0 %fusion.40 = f32[4,8,128]{2,1,0:T(8,128)S(1)} fusion(f32[4,1024,128,8]{2,1,3,0:T(8,128)S(1)} %get-tuple-element.282, f32[4,8,128]{2,1,0:T(8,128)S(1)} %get-tuple-element.283, pred[1024]{0:T(1024)(128)(4,1)S(1)} %broadcast_bitcast_fusion.2), kind=kLoop, calls=%fused_computation.8.clone.1 | loop fusion | flops 20967424 | bytes 16811008 | tf_op jit(solution)/shard_map/while/body/eval_jaxpr/reduce_sum | solution.py:45
  53.1 0.7 copy-done
  53.8 2.8 gather_fusion.1
  56.6 0.3 reshape.194
  56.9 8.2 %fusion.39 = f32[4,128,8,128]{3,1,2,0:T(8,128)S(1)} fusion(f32[4,1024,128,8]{2,1,3,0:T(8,128)} %copy-done, f32[4,8,128]{2,1,0:T(8,128)S(1)} %get-tuple-element.283, pred[1024]{0:T(1024)(128)(4,1)S(1)} %broadcast_bitcast_fusion.2, bf16[1024,4,128,1]{2,1,0,3:T(4,128)(2,1)S(1)} %bitcast.85), kind=kOutput, calls=%fused_computation.10.clone.1 | convolution fusion | flops 1094713344 | bytes 19940352 | tf_op jit(solution)/shard_map/while/body/eval_jaxpr/kgrs,skd->rkgd/dot_general | solution.py:46
  65.1 1.4 constant_dynamic-update-slice_fusion.2
  66.5 0.7 compare_and_fusion.2
  67.4 0.1 select_reduce_fusion.2
  67.6 2.8 gather_fusion
  70.4 0.3 reshape.193
  70.7 0.1 fusion.37
  70.9 1.3 constant_dynamic-slice_fusion.3
  72.2 3.1 bitcast_reduce_fusion.2
  75.3 5.0 %fusion.40 = f32[4,8,128]{2,1,0:T(8,128)S(1)} fusion(f32[4,1024,128,8]{2,1,3,0:T(8,128)S(1)} %get-tuple-element.282, f32[4,8,128]{2,1,0:T(8,128)S(1)} %get-tuple-element.283, pred[1024]{0:T(1024)(128)(4,1)S(1)} %broadcast_bitcast_fusion.2), kind=kLoop, calls=%fused_computation.8.clone.1 | loop fusion | flops 20967424 | bytes 16811008 | tf_op jit(solution)/shard_map/while/body/eval_jaxpr/reduce_sum | solution.py:45
  80.3 0.7 copy-done
  81.0 2.8 gather_fusion.1
  83.8 0.3 reshape.194
  84.1 8.2 %fusion.39 = f32[4,128,8,128]{3,1,2,0:T(8,128)S(1)} fusion(f32[4,1024,128,8]{2,1,3,0:T(8,128)} %copy-done, f32[4,8,128]{2,1,0:T(8,128)S(1)} %get-tuple-element.283, pred[1024]{0:T(1024)(128)(4,1)S(1)} %broadcast_bitcast_fusion.2, bf16[1024,4,128,1]{2,1,0,3:T(4,128)(2,1)S(1)} %bitcast.85), kind=kOutput, calls=%fused_computation.10.clone.1 | convolution fusion | flops 1094713344 | bytes 19940352 | tf_op jit(solution)/shard_map/while/body/eval_jaxpr/kgrs,skd->rkgd/dot_general | solution.py:46
  92.3 1.5 constant_dynamic-update-slice_fusion.2
  93.8 0.7 compare_and_fusion.2
  94.7 0.1 select_reduce_fusion.2
  94.8 2.8 gather_fusion
  97.7 0.3 reshape.193
  98.2 1.3 constant_dynamic-slice_fusion.3
  99.5 3.1 bitcast_reduce_fusion.2
  102.6 5.0 %fusion.40 = f32[4,8,128]{2,1,0:T(8,128)S(1)} fusion(f32[4,1024,128,8]{2,1,3,0:T(8,128)S(1)} %get-tuple-element.282, f32[4,8,128]{2,1,0:T(8,128)S(1)} %get-tuple-element.283, pred[1024]{0:T(1024)(128)(4,1)S(1)} %broadcast_bitcast_fusion.2), kind=kLoop, calls=%fused_computation.8.clone.1 | loop fusion | flops 20967424 | bytes 16811008 | tf_op jit(solution)/shard_map/while/body/eval_jaxpr/reduce_sum | solution.py:45
  107.6 0.7 copy-done
  108.3 2.8 gather_fusion.1
  111.1 0.3 reshape.194
  111.4 8.2 %fusion.39 = f32[4,128,8,128]{3,1,2,0:T(8,128)S(1)} fusion(f32[4,1024,128,8]{2,1,3,0:T(8,128)} %copy-done, f32[4,8,128]{2,1,0:T(8,128)S(1)} %get-tuple-element.283, pred[1024]{0:T(1024)(128)(4,1)S(1)} %broadcast_bitcast_fusion.2, bf16[1024,4,128,1]{2,1,0,3:T(4,128)(2,1)S(1)} %bitcast.85), kind=kOutput, calls=%fused_computation.10.clone.1 | convolution fusion | flops 1094713344 | bytes 19940352 | tf_op jit(solution)/shard_map/while/body/eval_jaxpr/kgrs,skd->rkgd/dot_general | solution.py:46
  119.6 1.5 constant_dynamic-update-slice_fusion.2
  121.1 11.8 %all_to_all.18 = f32[4,128,32]{1,2,0:T(8,128)S(1)} all-to-all(f32[4,128,32]{1,2,0:T(8,128)S(1)} %get-tuple-element.135), channel_id=1, replica_groups=mesh['groups'=2,'ctx'=4,'head'=2,'rep'=2] {'ctx'}, dimensions={0} | all-to-all | bytes 131072 | tf_op jit(solution)/shard_map/all_to_all | solution.py:65
  132.9 8.1 %all_to_all.19 = f32[4,128,32]{1,2,0:T(8,128)S(1)} all-to-all(f32[4,128,32]{1,2,0:T(8,128)S(1)} %get-tuple-element.136), channel_id=1, replica_groups=mesh['groups'=2,'ctx'=4,'head'=2,'rep'=2] {'ctx'}, dimensions={0} | all-to-all | bytes 131072 | tf_op jit(solution)/shard_map/all_to_all | solution.py:66
  141.0 5.7 %all-to-all-start = ((f32[4,128,4096]{1,2,0:T(8,128)}), f32[4,128,4096]{1,2,0:T(8,128)}, u32[]{:S(2)}, u32[]{:S(2)}) async-start(f32[4,128,4096]{1,2,0:T(8,128)} %get-tuple-element.134), calls=%async_computation | async-start | bytes 16777216 | tf_op jit(solution)/shard_map/all_to_all | solution.py:64
  146.8 180.7 %all-to-all-done = f32[4,128,4096]{1,2,0:T(8,128)} async-done(((f32[4,128,4096]{1,2,0:T(8,128)}), f32[4,128,4096]{1,2,0:T(8,128)}, u32[]{:S(2)}, u32[]{:S(2)}) %all-to-all-start) | async-done | bytes 8388640 | tf_op jit(solution)/shard_map/all_to_all | solution.py:64
  327.4 4.2 fusion.21
  331.6 1.1 fusion.22
  332.8 0.2 reduce-scatter.2.cloned.1.call-start
  333.0 79.6 %all-gather.2.cloned.1.call-done = bf16[512,4096]{0,1:T(8,128)(2,1)} async-done(((bf16[128,4096]{0,1:T(8,128)(2,1)}), bf16[512,4096]{0,1:T(8,128)(2,1)}) %all-gather.2.cloned.1.call-update) | async-done | bytes 4194320 | tf_op jit(solution)/shard_map/all_gather | solution.py:77
  412.6 14.9 %fusion.24 = f32[512,2048]{1,0:T(8,128)} fusion(bf16[512,4096]{0,1:T(8,128)(2,1)} %all-gather.2.cloned.1.call-done, bf16[4096,2048]{1,0:T(8,128)(2,1)} %param.11), kind=kOutput, calls=%fused_computation.44 | convolution fusion | flops 8589934592 | bytes 25165824 | tf_op jit(solution)/shard_map/dot_general | solution.py:76
  427.6 52.6 %reduce-scatter.2.cloned.1.call-done = f32[512,1024]{1,0:T(8,128)} async-done(((f32[512,2048]{1,0:T(8,128)}), f32[512,1024]{1,0:T(8,128)}) %reduce-scatter.2.cloned.1.call-update) | async-done | bytes 2097168 | tf_op jit(solution)/shard_map/reduce_scatter | solution.py:81
  480.2 2.7 convert_element_type.29
  (45 shorter events, 1.6 us)
Async XLA Ops:
  20.8 5.7 %copy-start = (f32[4,1024,128,8]{2,1,3,0:T(8,128)}, f32[4,1024,128,8]{2,1,3,0:T(8,128)S(1)}, u32[]{:S(2)}) copy-start(f32[4,1024,128,8]{2,1,3,0:T(8,128)S(1)} %get-tuple-element.282) | copy-start | bytes 50331652 | tf_op jit(solution)/shard_map/while
  48.1 5.7 %copy-start = (f32[4,1024,128,8]{2,1,3,0:T(8,128)}, f32[4,1024,128,8]{2,1,3,0:T(8,128)S(1)}, u32[]{:S(2)}) copy-start(f32[4,1024,128,8]{2,1,3,0:T(8,128)S(1)} %get-tuple-element.282) | copy-start | bytes 50331652 | tf_op jit(solution)/shard_map/while
  75.3 5.7 %copy-start = (f32[4,1024,128,8]{2,1,3,0:T(8,128)}, f32[4,1024,128,8]{2,1,3,0:T(8,128)S(1)}, u32[]{:S(2)}) copy-start(f32[4,1024,128,8]{2,1,3,0:T(8,128)S(1)} %get-tuple-element.282) | copy-start | bytes 50331652 | tf_op jit(solution)/shard_map/while
  102.6 5.7 %copy-start = (f32[4,1024,128,8]{2,1,3,0:T(8,128)}, f32[4,1024,128,8]{2,1,3,0:T(8,128)S(1)}, u32[]{:S(2)}) copy-start(f32[4,1024,128,8]{2,1,3,0:T(8,128)S(1)} %get-tuple-element.282) | copy-start | bytes 50331652 | tf_op jit(solution)/shard_map/while
  141.0 186.4 %all-to-all-start = ((f32[4,128,4096]{1,2,0:T(8,128)}), f32[4,128,4096]{1,2,0:T(8,128)}, u32[]{:S(2)}, u32[]{:S(2)}) async-start(f32[4,128,4096]{1,2,0:T(8,128)} %get-tuple-element.134), calls=%async_computation | async-start | bytes 16777216 | tf_op jit(solution)/shard_map/all_to_all | solution.py:64
  146.7 266.0 %all-gather.2.cloned.1.call-start = ((), (), s32[]{:S(2)}) async-start(), calls=%async_computation.4 | async-start | bytes 5242880 | tf_op jit(solution)/shard_map/all_gather | solution.py:77
  332.8 147.4 %reduce-scatter.2.cloned.1.call-start = ((), (), s32[]{:S(2)}) async-start(), calls=%async_computation.5 | async-start | bytes 6291456 | tf_op jit(solution)/shard_map/reduce_scatter | solution.py:81
Sparse Core Ops, SparseCore 0:
  332.9 79.6 all-gather.1
  427.7 52.4 reduce-scatter.1
where the time goes:
time: 491 us; the launch traced here: 490 us
  waiting for transfers between devices  313 us (64%)
  matrix products  60.1 us (12%)
  local copies, waits for them, and re-layouts  44.8 us (9%)
  other arithmetic  32.4 us (7%)
  blocking collectives  19.9 us (4%)
  between operations  13.4 us (3%)
  starting transfers between devices  5.92 us (1%)
    all_to_all x1, waiting for transfers between devices, shards(): lax.all_to_all(mixed_all, 'ctx', split_axis=0, concat_axis=0, tiled=True)  181 us
    all_gather x1, waiting for transfers between devices, shards(): lax.all_gather(attended, 'ctx', axis=0, tiled=True)  79.6 us
    reduce_scatter x1, waiting for transfers between devices, shards(): lax.psum_scatter(partial_out, 'head', scatter_dimension=1, tiled=True)  52.6 us
    dot_general x4, matrix products, attend(): jnp.einsum('kgrs,skd->rkgd', weights.astype(jnp.bfloat16), value_block, p...  32.7 us
    reduce_sum x4, other arithmetic, attend(): row_total = weights.sum(axis=-1)  19.9 us
    dot_general x1, matrix products, shards(): jnp.dot(lax.all_gather(attended, 'ctx', axis=0, tiled=True), out_weight,...  14.9 us
    dot_general x4, matrix products, attend(): jnp.einsum('rkgd,skd->kgrs', query_block, key_block, preferred_element_ty...  12.4 us
    all_to_all x1, blocking collectives, shards(): lax.all_to_all(top_all, 'ctx', split_axis=0, concat_axis=0, tiled=True)  11.8 us
  transfers between devices with their start and end apart: 3, of which 3 were waited for; matrix products, arithmetic and copies ran while one was open for 0% of the time, Pallas kernels for 0%

commit v1 on v0

v1 whole, which is shorter than its diff:
```python
import functools
import math

import jax
import jax.numpy as jnp
from jax import lax
from jax.experimental import pallas as pl
from jax.experimental.pallas import tpu as pltpu
from jax.sharding import PartitionSpec as P

HEADS = 64
KV_HEADS = 8
HEAD_DIM = 128
BLOCK = 128
CAP = 8
UNIT_HEADS = 2
GROUP = HEADS // KV_HEADS
PAIRS = GROUP // (2 * UNIT_HEADS)
UNIT = UNIT_HEADS * HEAD_DIM
NEG = -1e30
MESH = pl.DeviceIdType.MESH


def kernel(n, exchange, slots, q_hbm, k_hbm, v_hbm, pat_ref, w_hbm, out_ref,
           q_ref, k_ref, v_ref, w_ref, idx_ref, cnt_ref, kg_ref, vg_ref,
           own_o, own_s, send_o, send_s, left_o, left_s, right_o, right_s, res,
           acc, keep, xs, xr,
           load_sem, so_sem, ss_sem, lo_sem, ls_sem, ro_sem, rs_sem,
           res_recv, res_left, res_right, xs_sem, xr_sem):
    c = lax.axis_index("ctx")
    h = lax.axis_index("head")
    q_blocks = q_ref.shape[0]
    heads_kv = k_ref.shape[2] // HEAD_DIM
    local_blocks = k_ref.shape[0]
    per_block = heads_kv * PAIRS
    total = q_blocks * per_block
    width = w_ref.shape[1]
    share = width // 2
    roots = (max(n // 2 - 1, 0), n // 2)

    loads = [
        pltpu.make_async_copy(src, dst, load_sem.at[i])
        for i, (src, dst) in enumerate(
            ((k_hbm, k_ref), (v_hbm, v_ref), (q_hbm, q_ref), (w_hbm, w_ref))
        )
    ]
    for load in loads:
        load.start()

    barrier = pltpu.get_barrier_semaphore()

    @pl.when(c > 0)
    def _():
        pl.semaphore_signal(barrier, inc=1, device_id={"ctx": c - 1}, device_id_type=MESH)

    @pl.when(c < n - 1)
    def _():
        pl.semaphore_signal(barrier, inc=1, device_id={"ctx": c + 1}, device_id_type=MESH)

    if exchange:
        pl.semaphore_signal(barrier, inc=1, device_id={"head": 1 - h}, device_id_type=MESH)

    for b in range(q_blocks):
        count = jnp.int32(0)
        packed = [jnp.int32(0)] * CAP
        for j in range(pat_ref.shape[1]):
            local = pat_ref[b, j] - c * local_blocks
            inside = (local >= 0) & (local < local_blocks)
            for s in range(CAP):
                packed[s] = jnp.where(inside & (count == s), local, packed[s])
            count = count + inside.astype(jnp.int32)
        for s in range(CAP):
            idx_ref[b, s] = packed[s]
        cnt_ref[b] = count

    pl.semaphore_wait(barrier, (c > 0).astype(jnp.int32) + (c < n - 1).astype(jnp.int32) + int(exchange))
    loads[0].wait()
    loads[1].wait()
    loads[2].wait()

    scale = HEAD_DIM ** (-0.5) * math.log2(math.e)

    def up_copies(u, a, right):
        dst_o, dst_s = (left_o, left_s) if right else (right_o, right_s)
        rec_o, rec_s = (lo_sem, ls_sem) if right else (ro_sem, rs_sem)
        to = {"ctx": c + 1} if right else {"ctx": c - 1}
        return (
            pltpu.make_async_remote_copy(
                send_o.at[u, a], dst_o.at[u, a], so_sem.at[u, a], rec_o.at[u, a],
                device_id=to, device_id_type=MESH),
            pltpu.make_async_remote_copy(
                send_s.at[u, a], dst_s.at[u, a], ss_sem.at[u, a], rec_s.at[u, a],
                device_id=to, device_id_type=MESH),
        )

    def down_copy(u, a, right):
        return pltpu.make_async_remote_copy(
            res.at[u, a], res.at[u, a], (res_right if right else res_left).at[u, a],
            res_recv.at[u, a],
            device_id={"ctx": c + 1} if right else {"ctx": c - 1}, device_id_type=MESH)

    def x_copy(b):
        return pltpu.make_async_remote_copy(
            xs.at[b], xr.at[b], xs_sem.at[b], xr_sem.at[b],
            device_id={"head": 1 - h}, device_id_type=MESH)

    def attend(u):
        b = u // per_block
        k = (u // PAIRS) % heads_kv
        slot = u % slots

        @pl.when(u % PAIRS == 0)
        def _():
            column = pl.ds(pl.multiple_of(k * HEAD_DIM, HEAD_DIM), HEAD_DIM)
            for s in range(CAP):
                chosen = idx_ref[b, s]
                kg_ref[s * BLOCK:(s + 1) * BLOCK, :] = k_ref[chosen, :, column]
                vg_ref[s * BLOCK:(s + 1) * BLOCK, :] = v_ref[chosen, :, column]

        count = cnt_ref[b]
        for a in range(2):
            column = pl.multiple_of(((u % per_block) * 2 + a) * UNIT, UNIT)
            q = q_ref[b, :, pl.ds(column, UNIT)]
            q = jnp.concatenate(
                [q[:, i * HEAD_DIM:(i + 1) * HEAD_DIM] for i in range(UNIT_HEADS)], axis=0)
            scores = lax.dot_general(
                kg_ref[...], q, (((1,), (1,)), ((), ())), preferred_element_type=jnp.float32)
            parts = []
            for s in range(CAP):
                live = s < count
                parts.append(
                    scores[s * BLOCK:(s + 1) * BLOCK] * jnp.where(live, scale, 0.0)
                    + jnp.where(live, 0.0, NEG))
            scores = jnp.concatenate(parts, axis=0)
            top = jnp.max(scores, axis=0, keepdims=True)
            weights = jnp.exp2(scores - jnp.maximum(top, 0.1 * NEG))
            norm = jnp.sum(weights, axis=0, keepdims=True)
            own_o[slot, a] = lax.dot_general(
                vg_ref[...], weights.astype(jnp.bfloat16), (((0,), (0,)), ((), ())),
                preferred_element_type=jnp.float32)
            for i in range(UNIT_HEADS):
                lanes = slice(i * HEAD_DIM, (i + 1) * HEAD_DIM)
                own_s[slot, a, i:i + 1, :] = top[:, lanes]
                own_s[slot, a, UNIT_HEADS + i:UNIT_HEADS + i + 1, :] = norm[:, lanes]

    def fold(slot, a, got_o, got_s):
        mine = own_s[slot, a]
        m1, l1 = mine[:UNIT_HEADS], mine[UNIT_HEADS:2 * UNIT_HEADS]
        m2, l2 = got_s[:UNIT_HEADS], got_s[UNIT_HEADS:2 * UNIT_HEADS]
        top = jnp.maximum(m1, m2)
        f1, f2 = jnp.exp2(m1 - top), jnp.exp2(m2 - top)
        for i in range(UNIT_HEADS):
            lanes = slice(i * HEAD_DIM, (i + 1) * HEAD_DIM)
            own_o[slot, a, :, lanes] = (
                own_o[slot, a, :, lanes] * f1[i:i + 1]
                + got_o[:, lanes].astype(jnp.float32) * f2[i:i + 1])
        own_s[slot, a, :UNIT_HEADS, :] = top
        own_s[slot, a, UNIT_HEADS:2 * UNIT_HEADS, :] = l1 * f1 + l2 * f2

    def merge(u, a):
        root = roots[a]
        slot = u % slots

        @pl.when((c > 0) & (c <= root))
        def _():
            for copy in up_copies(u, a, True):
                copy.wait_recv()
            fold(slot, a, left_o[u, a], left_s[u, a])

        @pl.when((c < n - 1) & (c >= root))
        def _():
            for copy in up_copies(u, a, False):
                copy.wait_recv()
            fold(slot, a, right_o[u, a], right_s[u, a])

        @pl.when(c != root)
        def _():
            send_o[u, a] = own_o[slot, a].astype(jnp.bfloat16)
            send_s[u, a] = own_s[slot, a]

        @pl.when(c < root)
        def _():
            for copy in up_copies(u, a, True):
                copy.start()

        @pl.when(c > root)
        def _():
            for copy in up_copies(u, a, False):
                copy.start()

        @pl.when(c == root)
        def _():
            norm = own_s[slot, a, UNIT_HEADS:2 * UNIT_HEADS, :]
            for i in range(UNIT_HEADS):
                lanes = slice(i * HEAD_DIM, (i + 1) * HEAD_DIM)
                done = own_o[slot, a, :, lanes] / norm[i:i + 1]
                res[u, a, :, lanes] = done.T.astype(jnp.bfloat16)
            spread(u, a)

    def spread(u, a):
        @pl.when((c > 0) & (c <= roots[a]))
        def _():
            down_copy(u, a, False).start()

        @pl.when((c < n - 1) & (c >= roots[a]))
        def _():
            down_copy(u, a, True).start()

    def receive(u, a):
        @pl.when(c != roots[a])
        def _():
            down_copy(u, a, True).wait_recv()
            spread(u, a)

    def project(u):
        b = u // per_block
        lhs = jnp.concatenate([res[u, 0], res[u, 1]], axis=1)
        rows = pl.ds(pl.multiple_of((u % per_block) * 2 * UNIT, 2 * UNIT), 2 * UNIT)
        product = jnp.dot(lhs, w_ref[rows, :], preferred_element_type=jnp.float32)

        @pl.when(u % per_block == 0)
        def _():
            acc[...] = product

        @pl.when(u % per_block != 0)
        def _():
            acc[...] += product

        @pl.when(u % per_block == per_block - 1)
        def _():
            if exchange:
                mine = pl.multiple_of(h * share, 128)
                other = pl.multiple_of((1 - h) * share, 128)
                xs[b] = acc[:, pl.ds(other, share)].astype(jnp.bfloat16)
                x_copy(b).start()
                keep[b] = acc[:, pl.ds(mine, share)]
            else:
                out_ref[b] = acc[...]

    def span(far, root):
        return jnp.where(c < root, c, jnp.where(c > root, n - 1 - c, far))

    far = [max(r, n - 1 - r) for r in roots]
    merge_lag = [span(f, r) for f, r in zip(far, roots)]
    result_lag = [f + jnp.abs(c - r) for f, r in zip(far, roots)]
    last_lag = jnp.maximum(result_lag[0], result_lag[1])
    steps = total + max(f + max(r, n - 1 - r) for f, r in zip(far, roots))

    def step(t, carry):
        @pl.when(t < total)
        def _():
            attend(t)

        for a in range(2):
            u = t - merge_lag[a]

            @pl.when((u >= 0) & (u < total))
            def _(u=u, a=a):
                merge(u, a)

        for a in range(2):
            u = t - result_lag[a]

            @pl.when((u >= 0) & (u < total))
            def _(u=u, a=a):
                receive(u, a)

        u = t - last_lag

        @pl.when(t == 0)
        def _():
            loads[3].wait()

        @pl.when((u >= 0) & (u < total))
        def _():
            project(u)

        return carry

    lax.fori_loop(0, steps, step, 0)

    if exchange:
        for b in range(q_blocks):
            x_copy(b).wait_recv()
            out_ref[b] = (keep[b] + xr[b].astype(jnp.float32)).astype(out_ref.dtype)
            x_copy(b).wait_send()

    def drain(u, carry):
        for a in range(2):
            root = roots[a]

            @pl.when(c != root)
            def _():
                for copy in up_copies(u, a, True):
                    copy.wait_send()

            @pl.when((c > 0) & (c <= root))
            def _():
                down_copy(u, a, False).wait_send()

            @pl.when((c < n - 1) & (c >= root))
            def _():
                down_copy(u, a, True).wait_send()

        return carry

    lax.fori_loop(0, total, drain, 0)


def shards(n, n_head, queries, cached_keys, cached_values, pattern, out_weight):
    query_count, query_width = queries.shape
    q_blocks = query_count // BLOCK
    heads_kv = cached_keys.shape[1] // HEAD_DIM
    total = q_blocks * heads_kv * PAIRS
    width = out_weight.shape[1]
    share = width // 2
    exchange = n_head == 2 and share % 128 == 0
    slots = n // 2 + 1
    bf16, f32 = jnp.bfloat16, jnp.float32
    if exchange:
        out_shape = jax.ShapeDtypeStruct((q_blocks, BLOCK, share), bf16)
        x_rows = q_blocks
    else:
        out_shape = jax.ShapeDtypeStruct((q_blocks, BLOCK, width), f32)
        x_rows, share = 1, 128
    units = (total, 2)
    cache_shape = (cached_keys.shape[0] // BLOCK, BLOCK, cached_keys.shape[1])
    sem = pltpu.SemaphoreType.DMA
    any_space = pl.BlockSpec(memory_space=pl.ANY)
    out = pl.pallas_call(
        functools.partial(kernel, n, exchange, slots),
        out_shape=out_shape,
        in_specs=[any_space, any_space, any_space,
                  pl.BlockSpec(memory_space=pltpu.SMEM), any_space],
        out_specs=pl.BlockSpec(memory_space=pltpu.VMEM),
        scratch_shapes=[
            pltpu.VMEM((q_blocks, BLOCK, query_width), bf16),
            pltpu.VMEM(cache_shape, bf16),
            pltpu.VMEM(cache_shape, bf16),
            pltpu.VMEM(out_weight.shape, bf16),
            pltpu.SMEM((q_blocks, CAP), jnp.int32),
            pltpu.SMEM((q_blocks,), jnp.int32),
            pltpu.VMEM((CAP * BLOCK, HEAD_DIM), bf16),
            pltpu.VMEM((CAP * BLOCK, HEAD_DIM), bf16),
            pltpu.VMEM((slots, 2, HEAD_DIM, UNIT), f32),
            pltpu.VMEM((slots, 2, 8, BLOCK), f32),
            pltpu.VMEM(units + (HEAD_DIM, UNIT), bf16),
            pltpu.VMEM(units + (8, BLOCK), f32),
            pltpu.VMEM(units + (HEAD_DIM, UNIT), bf16),
            pltpu.VMEM(units + (8, BLOCK), f32),
            pltpu.VMEM(units + (HEAD_DIM, UNIT), bf16),
            pltpu.VMEM(units + (8, BLOCK), f32),
            pltpu.VMEM(units + (BLOCK, UNIT), bf16),
            pltpu.VMEM((BLOCK, width), f32),
            pltpu.VMEM((x_rows, BLOCK, share), f32),
            pltpu.VMEM((x_rows, BLOCK, share), bf16),
            pltpu.VMEM((x_rows, BLOCK, share), bf16),
            sem((4,)),
            sem(units), sem(units), sem(units), sem(units), sem(units), sem(units),
            sem(units), sem(units), sem(units),
            sem((x_rows,)), sem((x_rows,)),
        ],
        compiler_params=pltpu.CompilerParams(
            collective_id=0, has_side_effects=True, vmem_limit_bytes=60 * 1024 * 1024),
        cost_estimate=pl.CostEstimate(
            flops=4 * query_count * query_width * CAP * BLOCK
            + 2 * query_count * query_width * width,
            bytes_accessed=2 * (queries.size + 2 * cached_keys.size + out_weight.size),
            transcendentals=query_count * query_width * CAP),
    )(
        queries.reshape(q_blocks, BLOCK, query_width),
        cached_keys.reshape(cache_shape), cached_values.reshape(cache_shape), pattern, out_weight,
    )
    out = out.reshape(query_count, -1)
    if exchange:
        return out
    return lax.psum_scatter(out, "head", scatter_dimension=1, tiled=True).astype(bf16)


def solution(mesh):
    return jax.shard_map(
        functools.partial(shards, mesh.shape["ctx"], mesh.shape["head"]),
        mesh=mesh,
        in_specs=(
            P(("groups", "rep"), "head"),
            P(("groups", "ctx"), "head"),
            P(("groups", "ctx"), "head"),
            P(("groups", "rep"), None),
            P("head", "ctx"),
        ),
        out_specs=P(("groups", "rep"), ("ctx", "head")),
        check_vma=False,
    )
```

time: 491 us -> 162 us (0.33)
  waiting for transfers between devices: 313 us -> 0 us
  Pallas kernels: 0 us -> 160 us
  matrix products: 60.1 us -> 0 us
  local copies, waits for them, and re-layouts: 44.8 us -> 2.26 us
  other arithmetic: 32.4 us -> 0 us
  blocking collectives: 19.9 us -> 0 us
  between operations: 13.4 us -> 0.01 us
  starting transfers between devices: 5.92 us -> 0 us
    all_to_all x1 -> x0, waiting for transfers between devices: 181 us -> none  [shards(): lax.all_to_all(mixed_all, 'ctx', split_axis=0, concat_axis=0, tiled=True)]
    pallas_call x0 -> x1, Pallas kernels: none -> 160 us  [shards(): pl.pallas_call(functools.partial(kernel, n, exchange, slots), out_shape=o...]
    all_gather x1 -> x0, waiting for transfers between devices: 79.6 us -> none  [shards(): lax.all_gather(attended, 'ctx', axis=0, tiled=True)]
    dot_general x9 -> x0, matrix products: 60.1 us -> none  [the longest x4 32.7 us: attend(): jnp.einsum('kgrs,skd->rkgd', weights.astype(jnp.bfloat16), value_block, p...]
    reduce_scatter x1 -> x0, waiting for transfers between devices: 52.6 us -> none  [shards(): lax.psum_scatter(partial_out, 'head', scatter_dimension=1, tiled=True)]
    reduce_sum x10 -> x0, other arithmetic: 24.6 us -> none  [the longest x4 19.9 us: attend(): row_total = weights.sum(axis=-1)]
    gather x8 -> x0, local copies, waits for them, and re-layouts: 22.4 us -> none  [the longest x4 11.2 us: attend(): key_block = key_blocks[chosen].reshape(CAP * BLOCK, heads_kv, HEAD_DIM)]
    all_to_all x2 -> x0, blocking collectives: 19.9 us -> none  [the longest x1 11.8 us: shards(): lax.all_to_all(top_all, 'ctx', split_axis=0, concat_axis=0, tiled=True)]
  transfers between devices with their start and end apart: 3 -> 0, of which waited for: 3 -> 0; matrix products, arithmetic and copies ran while one was open for 0% -> 0% of each run, Pallas kernels for 0% -> 0%
where the time goes in v1:
time: 162 us
  Pallas kernels  160 us (99%)
  local copies, waits for them, and re-layouts  2.26 us (1%)
    pallas_call x1, Pallas kernels, shards(): pl.pallas_call(functools.partial(kernel, n, exchange, slots), out_shape=o...  160 us

profile of v1, /device:TPU:0, one launch (start us, length us, event | category | flops | bytes accessed | tf_op | source)
XLA Modules:
  0.0 162.3 jit_solution(3180404896327143772)
XLA Ops:
  0.0 160.0 %shard_map.55 = bf16[4,128,1024]{2,1,0:T(8,128)(2,1)} custom-call(bf16[4,128,4096]{2,1,0:T(8,128)(2,1)} %bitcast.5, bf16[32,128,512]{2,1,0:T(8,128)(2,1)} %bitcast.6, bf16[32,128,512]{2,1,0:T(8,128)(2,1)} %bitcast.7, s32[4,16]{1,0:T(4,128)} %pat_ref.1, bf16[4096,2048]{1,0:T(8,128)(2,1)} %w_hbm.1), custom_call_target="tpu_custom_call" | custom-call | flops 17179869184 | bytes 29360128 | tf_op jit(solution)/shard_map/pallas_call | solution.py:330
  160.0 2.3 %copy.7 = bf16[512,1024]{1,0:T(8,128)(2,1)} copy(bf16[512,1024]{1,0:T(8,128)(2,1)} %bitcast.4) | data formatting | bytes 2097152

commit v2 on v1

--- a/solution.py
+++ b/solution.py
@@ -18,6 +18,7 @@
 PAIRS = GROUP // (2 * UNIT_HEADS)
 UNIT = UNIT_HEADS * HEAD_DIM
 NEG = -1e30
+HOP = 2
 MESH = pl.DeviceIdType.MESH
 
 
@@ -25,7 +26,7 @@
            q_ref, k_ref, v_ref, w_ref, idx_ref, cnt_ref, kg_ref, vg_ref,
            own_o, own_s, send_o, send_s, left_o, left_s, right_o, right_s, res,
            acc, keep, xs, xr,
-           load_sem, so_sem, ss_sem, lo_sem, ls_sem, ro_sem, rs_sem,
+           cache_sem, q_sem, w_sem, so_sem, ss_sem, lo_sem, ls_sem, ro_sem, rs_sem,
            res_recv, res_left, res_right, xs_sem, xr_sem):
     c = lax.axis_index("ctx")
     h = lax.axis_index("head")
@@ -38,14 +39,26 @@
     share = width // 2
     roots = (max(n // 2 - 1, 0), n // 2)
 
-    loads = [
-        pltpu.make_async_copy(src, dst, load_sem.at[i])
-        for i, (src, dst) in enumerate(
-            ((k_hbm, k_ref), (v_hbm, v_ref), (q_hbm, q_ref), (w_hbm, w_ref))
-        )
-    ]
-    for load in loads:
+    cache_loads = (
+        pltpu.make_async_copy(k_hbm, k_ref, cache_sem.at[0]),
+        pltpu.make_async_copy(v_hbm, v_ref, cache_sem.at[1]),
+    )
+
+    def load_queries(b):
+        return pltpu.make_async_copy(q_hbm.at[b], q_ref.at[b], q_sem.at[b])
+
+    def load_weights(k):
+        rows = pl.ds(pl.multiple_of(k * GROUP * HEAD_DIM, GROUP * HEAD_DIM), GROUP * HEAD_DIM)
+        return pltpu.make_async_copy(w_hbm.at[rows], w_ref.at[rows], w_sem.at[k])
+
+    load_queries(0).start()
+    for load in cache_loads:
         load.start()
+    for b in range(1, q_blocks):
+        load_queries(b).start()
+    for k in range(heads_kv):
+        load_weights(k).start()
+    acc[...] = jnp.zeros_like(acc)
 
     barrier = pltpu.get_barrier_semaphore()
 
@@ -74,9 +87,9 @@
         cnt_ref[b] = count
 
     pl.semaphore_wait(barrier, (c > 0).astype(jnp.int32) + (c < n - 1).astype(jnp.int32) + int(exchange))
-    loads[0].wait()
-    loads[1].wait()
-    loads[2].wait()
+
+    for load in cache_loads:
+        load.wait()
 
     scale = HEAD_DIM ** (-0.5) * math.log2(math.e)
 
@@ -109,13 +122,17 @@
         k = (u // PAIRS) % heads_kv
         slot = u % slots
 
+        @pl.when(u % per_block == 0)
+        def _():
+            load_queries(b).wait()
+
         @pl.when(u % PAIRS == 0)
         def _():
             column = pl.ds(pl.multiple_of(k * HEAD_DIM, HEAD_DIM), HEAD_DIM)
             for s in range(CAP):
                 chosen = idx_ref[b, s]
                 kg_ref[s * BLOCK:(s + 1) * BLOCK, :] = k_ref[chosen, :, column]
-                vg_ref[s * BLOCK:(s + 1) * BLOCK, :] = v_ref[chosen, :, column]
+                vg_ref[:, s * BLOCK:(s + 1) * BLOCK] = v_ref[chosen, :, column].T
 
         count = cnt_ref[b]
         for a in range(2):
@@ -125,18 +142,18 @@
                 [q[:, i * HEAD_DIM:(i + 1) * HEAD_DIM] for i in range(UNIT_HEADS)], axis=0)
             scores = lax.dot_general(
                 kg_ref[...], q, (((1,), (1,)), ((), ())), preferred_element_type=jnp.float32)
-            parts = []
-            for s in range(CAP):
-                live = s < count
-                parts.append(
-                    scores[s * BLOCK:(s + 1) * BLOCK] * jnp.where(live, scale, 0.0)
-                    + jnp.where(live, 0.0, NEG))
-            scores = jnp.concatenate(parts, axis=0)
-            top = jnp.max(scores, axis=0, keepdims=True)
-            weights = jnp.exp2(scores - jnp.maximum(top, 0.1 * NEG))
-            norm = jnp.sum(weights, axis=0, keepdims=True)
-            own_o[slot, a] = lax.dot_general(
-                vg_ref[...], weights.astype(jnp.bfloat16), (((0,), (0,)), ((), ())),
+            slabs = [scores[s * BLOCK:(s + 1) * BLOCK] for s in range(CAP)]
+            top = jnp.full((1, UNIT), NEG, jnp.float32)
+            for s, slab in enumerate(slabs):
+                peak = jnp.max(slab, axis=0, keepdims=True) * scale
+                top = jnp.maximum(top, jnp.where(s < count, peak, NEG))
+            weights, norm = [], jnp.zeros((1, UNIT), jnp.float32)
+            for s, slab in enumerate(slabs):
+                weight = jnp.exp2(slab * scale - jnp.where(s < count, top, -NEG))
+                norm = norm + jnp.sum(weight, axis=0, keepdims=True)
+                weights.append(weight.astype(jnp.bfloat16))
+            own_o[slot, a] = jnp.dot(
+                vg_ref[...], jnp.concatenate(weights, axis=0),
                 preferred_element_type=jnp.float32)
             for i in range(UNIT_HEADS):
                 lanes = slice(i * HEAD_DIM, (i + 1) * HEAD_DIM)
@@ -212,19 +229,25 @@
             down_copy(u, a, True).wait_recv()
             spread(u, a)
 
+    def finish(b):
+        x_copy(b).wait_recv()
+        out_ref[b] = (keep[b] + xr[b].astype(jnp.float32)).astype(out_ref.dtype)
+
     def project(u):
         b = u // per_block
-        lhs = jnp.concatenate([res[u, 0], res[u, 1]], axis=1)
-        rows = pl.ds(pl.multiple_of((u % per_block) * 2 * UNIT, 2 * UNIT), 2 * UNIT)
-        product = jnp.dot(lhs, w_ref[rows, :], preferred_element_type=jnp.float32)
-
-        @pl.when(u % per_block == 0)
-        def _():
-            acc[...] = product
-
-        @pl.when(u % per_block != 0)
-        def _():
-            acc[...] += product
+        k = (u // PAIRS) % heads_kv
+
+        @pl.when(u < per_block)
+        def _():
+            load_weights(k).wait()
+
+        lhs = jnp.concatenate(
+            [res[u - PAIRS + 1 + i, a] for i in range(PAIRS) for a in range(2)], axis=1)
+        rows = pl.ds(pl.multiple_of(k * GROUP * HEAD_DIM, GROUP * HEAD_DIM), GROUP * HEAD_DIM)
+        tile = min(width, 512)
+        for start in range(0, width, tile):
+            lanes = slice(start, start + tile)
+            acc[:, lanes] += jnp.dot(lhs, w_ref[rows, lanes], preferred_element_type=jnp.float32)
 
         @pl.when(u % per_block == per_block - 1)
         def _():
@@ -234,17 +257,22 @@
                 xs[b] = acc[:, pl.ds(other, share)].astype(jnp.bfloat16)
                 x_copy(b).start()
                 keep[b] = acc[:, pl.ds(mine, share)]
+
+                @pl.when(b > 0)
+                def _():
+                    finish(b - 1)
             else:
                 out_ref[b] = acc[...]
+            acc[...] = jnp.zeros_like(acc)
 
     def span(far, root):
         return jnp.where(c < root, c, jnp.where(c > root, n - 1 - c, far))
 
     far = [max(r, n - 1 - r) for r in roots]
-    merge_lag = [span(f, r) for f, r in zip(far, roots)]
-    result_lag = [f + jnp.abs(c - r) for f, r in zip(far, roots)]
+    merge_lag = [HOP * span(f, r) for f, r in zip(far, roots)]
+    result_lag = [HOP * (f + jnp.abs(c - r)) for f, r in zip(far, roots)]
     last_lag = jnp.maximum(result_lag[0], result_lag[1])
-    steps = total + max(f + max(r, n - 1 - r) for f, r in zip(far, roots))
+    steps = total + HOP * max(f + max(r, n - 1 - r) for f, r in zip(far, roots))
 
     def step(t, carry):
         @pl.when(t < total)
@@ -267,11 +295,7 @@
 
         u = t - last_lag
 
-        @pl.when(t == 0)
-        def _():
-            loads[3].wait()
-
-        @pl.when((u >= 0) & (u < total))
+        @pl.when((u >= 0) & (u < total) & (u % PAIRS == PAIRS - 1))
         def _():
             project(u)
 
@@ -280,9 +304,8 @@
     lax.fori_loop(0, steps, step, 0)
 
     if exchange:
+        finish(q_blocks - 1)
         for b in range(q_blocks):
-            x_copy(b).wait_recv()
-            out_ref[b] = (keep[b] + xr[b].astype(jnp.float32)).astype(out_ref.dtype)
             x_copy(b).wait_send()
 
     def drain(u, carry):
@@ -315,7 +338,7 @@
     width = out_weight.shape[1]
     share = width // 2
     exchange = n_head == 2 and share % 128 == 0
-    slots = n // 2 + 1
+    slots = HOP * (n // 2) + 1
     bf16, f32 = jnp.bfloat16, jnp.float32
     if exchange:
         out_shape = jax.ShapeDtypeStruct((q_blocks, BLOCK, share), bf16)
@@ -341,7 +364,7 @@
             pltpu.SMEM((q_blocks, CAP), jnp.int32),
             pltpu.SMEM((q_blocks,), jnp.int32),
             pltpu.VMEM((CAP * BLOCK, HEAD_DIM), bf16),
-            pltpu.VMEM((CAP * BLOCK, HEAD_DIM), bf16),
+            pltpu.VMEM((HEAD_DIM, CAP * BLOCK), bf16),
             pltpu.VMEM((slots, 2, HEAD_DIM, UNIT), f32),
             pltpu.VMEM((slots, 2, 8, BLOCK), f32),
             pltpu.VMEM(units + (HEAD_DIM, UNIT), bf16),
@@ -355,7 +378,7 @@
             pltpu.VMEM((x_rows, BLOCK, share), f32),
             pltpu.VMEM((x_rows, BLOCK, share), bf16),
             pltpu.VMEM((x_rows, BLOCK, share), bf16),
-            sem((4,)),
+            sem((2,)), sem((q_blocks,)), sem((heads_kv,)),
             sem(units), sem(units), sem(units), sem(units), sem(units), sem(units),
             sem(units), sem(units), sem(units),
             sem((x_rows,)), sem((x_rows,)),

time: 162 us -> 138 us (0.85)
  Pallas kernels: 160 us -> 136 us
    pallas_call x1, Pallas kernels: 160 us -> 136 us  [shards(): pl.pallas_call(functools.partial(kernel, n, exchange, slots), out_shape=o...]
where the time goes in v2:
time: 138 us
  Pallas kernels  136 us (99%)
  local copies, waits for them, and re-layouts  2.26 us (2%)
    pallas_call x1, Pallas kernels, shards(): pl.pallas_call(functools.partial(kernel, n, exchange, slots), out_shape=o...  136 us

profile of v2, /device:TPU:0, one launch (start us, length us, event | category | flops | bytes accessed | tf_op | source)
XLA Modules:
  0.0 138.1 jit_solution(4241668650516749619)
XLA Ops:
  0.0 135.8 %shard_map.55 = bf16[4,128,1024]{2,1,0:T(8,128)(2,1)} custom-call(bf16[4,128,4096]{2,1,0:T(8,128)(2,1)} %bitcast.5, bf16[32,128,512]{2,1,0:T(8,128)(2,1)} %bitcast.6, bf16[32,128,512]{2,1,0:T(8,128)(2,1)} %bitcast.7, s32[4,16]{1,0:T(4,128)} %pat_ref.1, bf16[4096,2048]{1,0:T(8,128)(2,1)} %w_hbm.1), custom_call_target="tpu_custom_call" | custom-call | flops 17179869184 | bytes 29360128 | tf_op jit(solution)/shard_map/pallas_call | solution.py:353
  135.8 2.3 %copy.7 = bf16[512,1024]{1,0:T(8,128)(2,1)} copy(bf16[512,1024]{1,0:T(8,128)(2,1)} %bitcast.4) | data formatting | bytes 2097152

commit v3 on v2

--- a/solution.py
+++ b/solution.py
@@ -13,7 +13,7 @@
 HEAD_DIM = 128
 BLOCK = 128
 CAP = 8
-UNIT_HEADS = 2
+UNIT_HEADS = 4
 GROUP = HEADS // KV_HEADS
 PAIRS = GROUP // (2 * UNIT_HEADS)
 UNIT = UNIT_HEADS * HEAD_DIM

time: 138 us -> 142 us (1.029)
  Pallas kernels: 136 us -> 140 us
    pallas_call x1, Pallas kernels: 136 us -> 140 us  [shards(): pl.pallas_call(functools.partial(kernel, n, exchange, slots), out_shape=o...]
where the time goes in v3:
time: 142 us
  Pallas kernels  140 us (99%)
  local copies, waits for them, and re-layouts  2.26 us (2%)
    pallas_call x1, Pallas kernels, shards(): pl.pallas_call(functools.partial(kernel, n, exchange, slots), out_shape=o...  140 us

profile of v3, /device:TPU:0, one launch (start us, length us, event | category | flops | bytes accessed | tf_op | source)
XLA Modules:
  0.0 142.2 jit_solution(6881589780113533246)
XLA Ops:
  0.0 139.9 %shard_map.55 = bf16[4,128,1024]{2,1,0:T(8,128)(2,1)} custom-call(bf16[4,128,4096]{2,1,0:T(8,128)(2,1)} %bitcast.5, bf16[32,128,512]{2,1,0:T(8,128)(2,1)} %bitcast.6, bf16[32,128,512]{2,1,0:T(8,128)(2,1)} %bitcast.7, s32[4,16]{1,0:T(4,128)} %pat_ref.1, bf16[4096,2048]{1,0:T(8,128)(2,1)} %w_hbm.1), custom_call_target="tpu_custom_call" | custom-call | flops 17179869184 | bytes 29360128 | tf_op jit(solution)/shard_map/pallas_call | solution.py:353
  139.9 2.3 %copy.7 = bf16[512,1024]{1,0:T(8,128)(2,1)} copy(bf16[512,1024]{1,0:T(8,128)(2,1)} %bitcast.4) | data formatting | bytes 2097152

commit v4 on v2

--- a/solution.py
+++ b/solution.py
@@ -117,10 +117,9 @@
             xs.at[b], xr.at[b], xs_sem.at[b], xr_sem.at[b],
             device_id={"head": 1 - h}, device_id_type=MESH)
 
-    def attend(u):
+    def prepare(u):
         b = u // per_block
         k = (u // PAIRS) % heads_kv
-        slot = u % slots
 
         @pl.when(u % per_block == 0)
         def _():
@@ -134,7 +133,16 @@
                 kg_ref[s * BLOCK:(s + 1) * BLOCK, :] = k_ref[chosen, :, column]
                 vg_ref[:, s * BLOCK:(s + 1) * BLOCK] = v_ref[chosen, :, column].T
 
+    def attend(u, beside):
+        b = u // per_block
+        slot = u % slots
         count = cnt_ref[b]
+        beside = list(beside)
+
+        def turn():
+            if beside:
+                beside.pop(0)()
+
         for a in range(2):
             column = pl.multiple_of(((u % per_block) * 2 + a) * UNIT, UNIT)
             q = q_ref[b, :, pl.ds(column, UNIT)]
@@ -142,6 +150,7 @@
                 [q[:, i * HEAD_DIM:(i + 1) * HEAD_DIM] for i in range(UNIT_HEADS)], axis=0)
             scores = lax.dot_general(
                 kg_ref[...], q, (((1,), (1,)), ((), ())), preferred_element_type=jnp.float32)
+            turn()
             slabs = [scores[s * BLOCK:(s + 1) * BLOCK] for s in range(CAP)]
             top = jnp.full((1, UNIT), NEG, jnp.float32)
             for s, slab in enumerate(slabs):
@@ -152,6 +161,7 @@
                 weight = jnp.exp2(slab * scale - jnp.where(s < count, top, -NEG))
                 norm = norm + jnp.sum(weight, axis=0, keepdims=True)
                 weights.append(weight.astype(jnp.bfloat16))
+            turn()
             own_o[slot, a] = jnp.dot(
                 vg_ref[...], jnp.concatenate(weights, axis=0),
                 preferred_element_type=jnp.float32)
@@ -159,95 +169,118 @@
                 lanes = slice(i * HEAD_DIM, (i + 1) * HEAD_DIM)
                 own_s[slot, a, i:i + 1, :] = top[:, lanes]
                 own_s[slot, a, UNIT_HEADS + i:UNIT_HEADS + i + 1, :] = norm[:, lanes]
-
-    def fold(slot, a, got_o, got_s):
-        mine = own_s[slot, a]
-        m1, l1 = mine[:UNIT_HEADS], mine[UNIT_HEADS:2 * UNIT_HEADS]
-        m2, l2 = got_s[:UNIT_HEADS], got_s[UNIT_HEADS:2 * UNIT_HEADS]
-        top = jnp.maximum(m1, m2)
-        f1, f2 = jnp.exp2(m1 - top), jnp.exp2(m2 - top)
+        while beside:
+            turn()
+
+    def combine(parts):
+        stats = [stat for _, stat in parts]
+        tops = [stat[:UNIT_HEADS] for stat in stats]
+        top = functools.reduce(jnp.maximum, tops)
+        factors = [jnp.exp2(one - top) for one in tops]
+        norm = sum(stat[UNIT_HEADS:] * f for stat, f in zip(stats, factors))
+        heads = []
         for i in range(UNIT_HEADS):
             lanes = slice(i * HEAD_DIM, (i + 1) * HEAD_DIM)
-            own_o[slot, a, :, lanes] = (
-                own_o[slot, a, :, lanes] * f1[i:i + 1]
-                + got_o[:, lanes].astype(jnp.float32) * f2[i:i + 1])
-        own_s[slot, a, :UNIT_HEADS, :] = top
-        own_s[slot, a, UNIT_HEADS:2 * UNIT_HEADS, :] = l1 * f1 + l2 * f2
+            heads.append(sum(
+                out[:, lanes].astype(jnp.float32) * f[i:i + 1]
+                for (out, _), f in zip(parts, factors)))
+        return heads, top, norm
 
     def merge(u, a):
         root = roots[a]
         slot = u % slots
 
-        @pl.when((c > 0) & (c <= root))
-        def _():
-            for copy in up_copies(u, a, True):
+        def arrived(right):
+            for copy in up_copies(u, a, right):
                 copy.wait_recv()
-            fold(slot, a, left_o[u, a], left_s[u, a])
-
-        @pl.when((c < n - 1) & (c >= root))
-        def _():
-            for copy in up_copies(u, a, False):
-                copy.wait_recv()
-            fold(slot, a, right_o[u, a], right_s[u, a])
-
-        @pl.when(c != root)
-        def _():
-            send_o[u, a] = own_o[slot, a].astype(jnp.bfloat16)
-            send_s[u, a] = own_s[slot, a]
+            if right:
+                return left_o[u, a], left_s[u, a]
+            return right_o[u, a], right_s[u, a]
+
+        def pass_on(right):
+            first = c == 0 if right else c == n - 1
+
+            @pl.when(first)
+            def _():
+                send_o[u, a] = own_o[slot, a].astype(jnp.bfloat16)
+                send_s[u, a] = own_s[slot, a]
+                for copy in up_copies(u, a, right):
+                    copy.start()
+
+            @pl.when(jnp.logical_not(first))
+            def _():
+                got = arrived(right)
+                heads, top, norm = combine([(own_o[slot, a], own_s[slot, a]), got])
+                for i in range(UNIT_HEADS):
+                    lanes = slice(i * HEAD_DIM, (i + 1) * HEAD_DIM)
+                    send_o[u, a, :, lanes] = heads[i].astype(jnp.bfloat16)
+                send_s[u, a, :UNIT_HEADS, :] = top
+                send_s[u, a, UNIT_HEADS:, :] = norm
+                for copy in up_copies(u, a, right):
+                    copy.start()
 
         @pl.when(c < root)
         def _():
-            for copy in up_copies(u, a, True):
-                copy.start()
+            pass_on(True)
 
         @pl.when(c > root)
         def _():
-            for copy in up_copies(u, a, False):
-                copy.start()
+            pass_on(False)
 
         @pl.when(c == root)
         def _():
-            norm = own_s[slot, a, UNIT_HEADS:2 * UNIT_HEADS, :]
+            parts = [(own_o[slot, a], own_s[slot, a])]
+            if root > 0:
+                parts.append(arrived(True))
+            if root < n - 1:
+                parts.append(arrived(False))
+            heads, _, norm = combine(parts)
+            inverse = 1.0 / norm
             for i in range(UNIT_HEADS):
                 lanes = slice(i * HEAD_DIM, (i + 1) * HEAD_DIM)
-                done = own_o[slot, a, :, lanes] / norm[i:i + 1]
-                res[u, a, :, lanes] = done.T.astype(jnp.bfloat16)
-            spread(u, a)
-
-    def spread(u, a):
-        @pl.when((c > 0) & (c <= roots[a]))
-        def _():
-            down_copy(u, a, False).start()
-
-        @pl.when((c < n - 1) & (c >= roots[a]))
-        def _():
-            down_copy(u, a, True).start()
+                res[u, a, :, lanes] = (heads[i] * inverse[i:i + 1]).T.astype(jnp.bfloat16)
+            if root > 0:
+                down_copy(u, a, False).start()
+            if root < n - 1:
+                down_copy(u, a, True).start()
 
     def receive(u, a):
         @pl.when(c != roots[a])
         def _():
             down_copy(u, a, True).wait_recv()
-            spread(u, a)
+
+            @pl.when((c > 0) & (c < roots[a]))
+            def _():
+                down_copy(u, a, False).start()
+
+            @pl.when((c < n - 1) & (c > roots[a]))
+            def _():
+                down_copy(u, a, True).start()
 
     def finish(b):
         x_copy(b).wait_recv()
         out_ref[b] = (keep[b] + xr[b].astype(jnp.float32)).astype(out_ref.dtype)
 
+    def await_weights(u):
+        @pl.when(u < per_block)
+        def _():
+            load_weights((u // PAIRS) % heads_kv).wait()
+
     def project(u):
-        b = u // per_block
         k = (u // PAIRS) % heads_kv
-
-        @pl.when(u < per_block)
-        def _():
-            load_weights(k).wait()
-
-        lhs = jnp.concatenate(
-            [res[u - PAIRS + 1 + i, a] for i in range(PAIRS) for a in range(2)], axis=1)
         rows = pl.ds(pl.multiple_of(k * GROUP * HEAD_DIM, GROUP * HEAD_DIM), GROUP * HEAD_DIM)
         tile = min(width, 512)
-        for start in range(0, width, tile):
+
+        def one(start):
             lanes = slice(start, start + tile)
+            lhs = jnp.concatenate(
+                [res[u - PAIRS + 1 + i, a] for i in range(PAIRS) for a in range(2)], axis=1)
             acc[:, lanes] += jnp.dot(lhs, w_ref[rows, lanes], preferred_element_type=jnp.float32)
+
+        return [functools.partial(one, start) for start in range(0, width, tile)]
+
+    def close(u):
+        b = u // per_block
 
         @pl.when(u % per_block == per_block - 1)
         def _():
@@ -272,12 +305,33 @@
     merge_lag = [HOP * span(f, r) for f, r in zip(far, roots)]
     result_lag = [HOP * (f + jnp.abs(c - r)) for f, r in zip(far, roots)]
     last_lag = jnp.maximum(result_lag[0], result_lag[1])
-    steps = total + HOP * max(f + max(r, n - 1 - r) for f, r in zip(far, roots))
+    steps = total + 1 + HOP * max(f + max(r, n - 1 - r) for f, r in zip(far, roots))
 
     def step(t, carry):
-        @pl.when(t < total)
-        def _():
-            attend(t)
+        done = t - last_lag - 1
+        attending = t < total
+        projecting = (done >= 0) & (done < total) & (done % PAIRS == PAIRS - 1)
+
+        @pl.when(attending)
+        def _():
+            prepare(t)
+
+        @pl.when(projecting)
+        def _():
+            await_weights(done)
+
+        @pl.when(attending & projecting)
+        def _():
+            attend(t, project(done))
+
+        @pl.when(attending & jnp.logical_not(projecting))
+        def _():
+            attend(t, [])
+
+        @pl.when(jnp.logical_not(attending) & projecting)
+        def _():
+            for one in project(done):
+                one()
 
         for a in range(2):
             u = t - merge_lag[a]
@@ -286,18 +340,16 @@
             def _(u=u, a=a):
                 merge(u, a)
 
+        @pl.when(projecting)
+        def _():
+            close(done)
+
         for a in range(2):
             u = t - result_lag[a]
 
             @pl.when((u >= 0) & (u < total))
             def _(u=u, a=a):
                 receive(u, a)
-
-        u = t - last_lag
-
-        @pl.when((u >= 0) & (u < total) & (u % PAIRS == PAIRS - 1))
-        def _():
-            project(u)
 
         return carry
 
@@ -366,13 +418,13 @@
             pltpu.VMEM((CAP * BLOCK, HEAD_DIM), bf16),
             pltpu.VMEM((HEAD_DIM, CAP * BLOCK), bf16),
             pltpu.VMEM((slots, 2, HEAD_DIM, UNIT), f32),
-            pltpu.VMEM((slots, 2, 8, BLOCK), f32),
+            pltpu.VMEM((slots, 2, 2 * UNIT_HEADS, BLOCK), f32),
             pltpu.VMEM(units + (HEAD_DIM, UNIT), bf16),
-            pltpu.VMEM(units + (8, BLOCK), f32),
+            pltpu.VMEM(units + (2 * UNIT_HEADS, BLOCK), f32),
             pltpu.VMEM(units + (HEAD_DIM, UNIT), bf16),
-            pltpu.VMEM(units + (8, BLOCK), f32),
+            pltpu.VMEM(units + (2 * UNIT_HEADS, BLOCK), f32),
             pltpu.VMEM(units + (HEAD_DIM, UNIT), bf16),
-            pltpu.VMEM(units + (8, BLOCK), f32),
+            pltpu.VMEM(units + (2 * UNIT_HEADS, BLOCK), f32),
             pltpu.VMEM(units + (BLOCK, UNIT), bf16),
             pltpu.VMEM((BLOCK, width), f32),
             pltpu.VMEM((x_rows, BLOCK, share), f32),

time: 138 us -> 135 us (0.978)
  Pallas kernels: 136 us -> 132 us
    pallas_call x1, Pallas kernels: 136 us -> 132 us  [shards(): pl.pallas_call(functools.partial(kernel, n, exchange, slots), out_shape=o...]
where the time goes in v4:
time: 135 us
  Pallas kernels  132 us (98%)
  local copies, waits for them, and re-layouts  2.26 us (2%)
    pallas_call x1, Pallas kernels, shards(): pl.pallas_call(functools.partial(kernel, n, exchange, slots), out_shape=o...  132 us

profile of v4, /device:TPU:0, one launch (start us, length us, event | category | flops | bytes accessed | tf_op | source)
XLA Modules:
  0.0 134.8 jit_solution(16685118638664929549)
XLA Ops:
  0.0 132.5 %shard_map.55 = bf16[4,128,1024]{2,1,0:T(8,128)(2,1)} custom-call(bf16[4,128,4096]{2,1,0:T(8,128)(2,1)} %bitcast.5, bf16[32,128,512]{2,1,0:T(8,128)(2,1)} %bitcast.6, bf16[32,128,512]{2,1,0:T(8,128)(2,1)} %bitcast.7, s32[4,16]{1,0:T(4,128)} %pat_ref.1, bf16[4096,2048]{1,0:T(8,128)(2,1)} %w_hbm.1), custom_call_target="tpu_custom_call" | custom-call | flops 17179869184 | bytes 29360128 | tf_op jit(solution)/shard_map/pallas_call | solution.py:405
  132.5 2.3 %copy.7 = bf16[512,1024]{1,0:T(8,128)(2,1)} copy(bf16[512,1024]{1,0:T(8,128)(2,1)} %bitcast.4) | data formatting | bytes 2097152

commit v5 on v4

--- a/solution.py
+++ b/solution.py
@@ -18,7 +18,7 @@
 PAIRS = GROUP // (2 * UNIT_HEADS)
 UNIT = UNIT_HEADS * HEAD_DIM
 NEG = -1e30
-HOP = 2
+HOP = 1
 MESH = pl.DeviceIdType.MESH
 
 
@@ -133,7 +133,7 @@
                 kg_ref[s * BLOCK:(s + 1) * BLOCK, :] = k_ref[chosen, :, column]
                 vg_ref[:, s * BLOCK:(s + 1) * BLOCK] = v_ref[chosen, :, column].T
 
-    def attend(u, beside):
+    def attend(u, a, beside):
         b = u // per_block
         slot = u % slots
         count = cnt_ref[b]
@@ -143,32 +143,31 @@
             if beside:
                 beside.pop(0)()
 
-        for a in range(2):
-            column = pl.multiple_of(((u % per_block) * 2 + a) * UNIT, UNIT)
-            q = q_ref[b, :, pl.ds(column, UNIT)]
-            q = jnp.concatenate(
-                [q[:, i * HEAD_DIM:(i + 1) * HEAD_DIM] for i in range(UNIT_HEADS)], axis=0)
-            scores = lax.dot_general(
-                kg_ref[...], q, (((1,), (1,)), ((), ())), preferred_element_type=jnp.float32)
-            turn()
-            slabs = [scores[s * BLOCK:(s + 1) * BLOCK] for s in range(CAP)]
-            top = jnp.full((1, UNIT), NEG, jnp.float32)
-            for s, slab in enumerate(slabs):
-                peak = jnp.max(slab, axis=0, keepdims=True) * scale
-                top = jnp.maximum(top, jnp.where(s < count, peak, NEG))
-            weights, norm = [], jnp.zeros((1, UNIT), jnp.float32)
-            for s, slab in enumerate(slabs):
-                weight = jnp.exp2(slab * scale - jnp.where(s < count, top, -NEG))
-                norm = norm + jnp.sum(weight, axis=0, keepdims=True)
-                weights.append(weight.astype(jnp.bfloat16))
-            turn()
-            own_o[slot, a] = jnp.dot(
-                vg_ref[...], jnp.concatenate(weights, axis=0),
-                preferred_element_type=jnp.float32)
-            for i in range(UNIT_HEADS):
-                lanes = slice(i * HEAD_DIM, (i + 1) * HEAD_DIM)
-                own_s[slot, a, i:i + 1, :] = top[:, lanes]
-                own_s[slot, a, UNIT_HEADS + i:UNIT_HEADS + i + 1, :] = norm[:, lanes]
+        column = pl.multiple_of(((u % per_block) * 2 + a) * UNIT, UNIT)
+        q = q_ref[b, :, pl.ds(column, UNIT)]
+        q = jnp.concatenate(
+            [q[:, i * HEAD_DIM:(i + 1) * HEAD_DIM] for i in range(UNIT_HEADS)], axis=0)
+        scores = lax.dot_general(
+            kg_ref[...], q, (((1,), (1,)), ((), ())), preferred_element_type=jnp.float32)
+        turn()
+        slabs = [scores[s * BLOCK:(s + 1) * BLOCK] for s in range(CAP)]
+        top = jnp.full((1, UNIT), NEG, jnp.float32)
+        for s, slab in enumerate(slabs):
+            peak = jnp.max(slab, axis=0, keepdims=True) * scale
+            top = jnp.maximum(top, jnp.where(s < count, peak, NEG))
+        weights, norm = [], jnp.zeros((1, UNIT), jnp.float32)
+        for s, slab in enumerate(slabs):
+            weight = jnp.exp2(slab * scale - jnp.where(s < count, top, -NEG))
+            norm = norm + jnp.sum(weight, axis=0, keepdims=True)
+            weights.append(weight.astype(jnp.bfloat16))
+        turn()
+        own_o[slot, a] = jnp.dot(
+            vg_ref[...], jnp.concatenate(weights, axis=0),
+            preferred_element_type=jnp.float32)
+        for i in range(UNIT_HEADS):
+            lanes = slice(i * HEAD_DIM, (i + 1) * HEAD_DIM)
+            own_s[slot, a, i:i + 1, :] = top[:, lanes]
+            own_s[slot, a, UNIT_HEADS + i:UNIT_HEADS + i + 1, :] = norm[:, lanes]
         while beside:
             turn()
 
@@ -320,31 +319,36 @@
         def _():
             await_weights(done)
 
-        @pl.when(attending & projecting)
-        def _():
-            attend(t, project(done))
-
-        @pl.when(attending & jnp.logical_not(projecting))
-        def _():
-            attend(t, [])
-
-        @pl.when(jnp.logical_not(attending) & projecting)
-        def _():
-            for one in project(done):
-                one()
-
         for a in range(2):
+            def tiles(a=a):
+                tiles = project(done)
+                middle = len(tiles) // 2
+                return tiles[middle:] if a else tiles[:middle]
+
+            @pl.when(attending & projecting)
+            def _(a=a, tiles=tiles):
+                attend(t, a, tiles())
+
+            @pl.when(attending & jnp.logical_not(projecting))
+            def _(a=a):
+                attend(t, a, [])
+
+            @pl.when(jnp.logical_not(attending) & projecting)
+            def _(tiles=tiles):
+                for one in tiles():
+                    one()
+
             u = t - merge_lag[a]
 
             @pl.when((u >= 0) & (u < total))
             def _(u=u, a=a):
                 merge(u, a)
 
-        @pl.when(projecting)
-        def _():
-            close(done)
-
-        for a in range(2):
+            if a == 1:
+                @pl.when(projecting)
+                def _():
+                    close(done)
+
             u = t - result_lag[a]
 
             @pl.when((u >= 0) & (u < total))

time: 135 us -> 152 us (1.13)
  Pallas kernels: 132 us -> 150 us
    pallas_call x1, Pallas kernels: 132 us -> 150 us  [shards(): pl.pallas_call(functools.partial(kernel, n, exchange, slots), out_shape=o...]
where the time goes in v5:
time: 152 us
  Pallas kernels  150 us (99%)
  local copies, waits for them, and re-layouts  2.26 us (1%)
    pallas_call x1, Pallas kernels, shards(): pl.pallas_call(functools.partial(kernel, n, exchange, slots), out_shape=o...  150 us

profile of v5, /device:TPU:0, one launch (start us, length us, event | category | flops | bytes accessed | tf_op | source)
XLA Modules:
  0.0 151.8 jit_solution(10604999424209682138)
XLA Ops:
  0.0 149.5 %shard_map.55 = bf16[4,128,1024]{2,1,0:T(8,128)(2,1)} custom-call(bf16[4,128,4096]{2,1,0:T(8,128)(2,1)} %bitcast.5, bf16[32,128,512]{2,1,0:T(8,128)(2,1)} %bitcast.6, bf16[32,128,512]{2,1,0:T(8,128)(2,1)} %bitcast.7, s32[4,16]{1,0:T(4,128)} %pat_ref.1, bf16[4096,2048]{1,0:T(8,128)(2,1)} %w_hbm.1), custom_call_target="tpu_custom_call" | custom-call | flops 17179869184 | bytes 29360128 | tf_op jit(solution)/shard_map/pallas_call | solution.py:409
  149.5 2.3 %copy.7 = bf16[512,1024]{1,0:T(8,128)(2,1)} copy(bf16[512,1024]{1,0:T(8,128)(2,1)} %bitcast.4) | data formatting | bytes 2097152

commit v6 on v5

--- a/solution.py
+++ b/solution.py
@@ -18,7 +18,7 @@
 PAIRS = GROUP // (2 * UNIT_HEADS)
 UNIT = UNIT_HEADS * HEAD_DIM
 NEG = -1e30
-HOP = 1
+HOP = 2
 MESH = pl.DeviceIdType.MESH
 
 

time: 152 us -> 134 us (0.88)
  Pallas kernels: 150 us -> 132 us
    pallas_call x1, Pallas kernels: 150 us -> 132 us  [shards(): pl.pallas_call(functools.partial(kernel, n, exchange, slots), out_shape=o...]
where the time goes in v6:
time: 134 us
  Pallas kernels  132 us (99%)
  local copies, waits for them, and re-layouts  2.26 us (2%)
    pallas_call x1, Pallas kernels, shards(): pl.pallas_call(functools.partial(kernel, n, exchange, slots), out_shape=o...  132 us

profile of v6, /device:TPU:0, one launch (start us, length us, event | category | flops | bytes accessed | tf_op | source)
XLA Modules:
  0.0 134.0 jit_solution(14520027477977948157)
XLA Ops:
  0.0 131.8 %shard_map.55 = bf16[4,128,1024]{2,1,0:T(8,128)(2,1)} custom-call(bf16[4,128,4096]{2,1,0:T(8,128)(2,1)} %bitcast.5, bf16[32,128,512]{2,1,0:T(8,128)(2,1)} %bitcast.6, bf16[32,128,512]{2,1,0:T(8,128)(2,1)} %bitcast.7, s32[4,16]{1,0:T(4,128)} %pat_ref.1, bf16[4096,2048]{1,0:T(8,128)(2,1)} %w_hbm.1), custom_call_target="tpu_custom_call" | custom-call | flops 17179869184 | bytes 29360128 | tf_op jit(solution)/shard_map/pallas_call | solution.py:409
  131.8 2.3 %copy.7 = bf16[512,1024]{1,0:T(8,128)(2,1)} copy(bf16[512,1024]{1,0:T(8,128)(2,1)} %bitcast.4) | data formatting | bytes 2097152
